TPU v7x, 32 devices: a whole 2x2x4 slice. The times are simulated.
32 devices in a mesh: tgt: 32 (over z, y, x, core), src: 1.
Axes of the slice: x: 2, y: 2, z: 4, core: 2. Of those that a mesh axis runs over, the one named last changes fastest.
Arguments:
- connectome: bfloat16 [4096, 51200], P('tgt', 'src'), may hold values from -0.02734375 to 0.02734375
- history: bfloat16 [32, 32, 51200], P('tgt', None, 'src'), may hold values from 0 to 5
- delays: int32 [32, 400], P('tgt', 'src'), may hold values from 16 to 32
- cycle_head: int32 [1], replicated, may hold values from 0 to 31
- outside_afferent: float32 [32], replicated, may hold values from 120 to 320
- init_state: float32 [6, 32, 4096], P(None, None, 'tgt'), may hold values from -4 to 4
- lead_field: bfloat16 [4096, 256], P('tgt'), may hold values from -0.09375 to 0.09375
Outputs:
- sensor_signal: float32 [32, 16, 256], P('tgt')
- final_state: float32 [6, 32, 4096], P(None, None, ('tgt', 'src'))
Inputs may be any that keep to these rules, and one draw needn't show every extreme that they name: `cycle_head`: a slot of the history cycle.
All inputs are finite; a program needn't handle non-finite values.
Results may differ from a plain program's by a relative error of at most 0.003.
Values may be sent and summed in bfloat16 or wider, within the bound.
A program may use at most 320 MiB of HBM per device.

v0:
```python
import jax
import jax.numpy as jnp
from jax import lax
from jax.sharding import PartitionSpec as P

STEPS = 16


integrator_step_width = 0.1
positive_synaptic_amplitude = 0.0325
negative_synaptic_amplitude = 0.11
interneuron_fraction = 0.5
global_link_scale = 30.0
stellate_contact_count = 135.0
recurrent_loop_contacts = 108.0
interneuron_contact_count = 33.75
peak_spike_rate = 5.0
logistic_slope_factor = 0.56
logistic_midpoint = 6.0


def spike_rate_response(cell_depolarization):
    return peak_spike_rate * jax.nn.sigmoid(
        logistic_slope_factor * (cell_depolarization - logistic_midpoint)
    )


def advance(carry, applied_stimulus, outside_afferent):
    (
        principal_cell_depolarization,
        stellate_mean_depolarization,
        interneuron_mean_depolarization,
        principal_cell_slope,
        excite_rate,
        interneuron_slope,
    ) = carry
    next_principal_cell_slope = principal_cell_slope + integrator_step_width * (
        positive_synaptic_amplitude
        * spike_rate_response(stellate_mean_depolarization - interneuron_mean_depolarization)
        - 2.0 * principal_cell_slope
        - principal_cell_depolarization
    )
    summed_afferent_rate = (
        outside_afferent[:, None]
        + recurrent_loop_contacts
        * spike_rate_response(stellate_contact_count * principal_cell_depolarization)
        + global_link_scale * applied_stimulus
    )
    new_excite_rate = excite_rate + integrator_step_width * (
        positive_synaptic_amplitude * summed_afferent_rate
        - 2.0 * excite_rate
        - stellate_mean_depolarization
    )
    next_interneuron_slope = interneuron_slope + integrator_step_width * (
        negative_synaptic_amplitude
        * interneuron_contact_count
        * spike_rate_response(interneuron_contact_count * principal_cell_depolarization)
        - 2.0 * interneuron_fraction * interneuron_slope
        - interneuron_fraction * interneuron_fraction * interneuron_mean_depolarization
    )
    return (
        principal_cell_depolarization + integrator_step_width * principal_cell_slope,
        stellate_mean_depolarization + integrator_step_width * excite_rate,
        interneuron_mean_depolarization + integrator_step_width * interneuron_slope,
        next_principal_cell_slope,
        new_excite_rate,
        next_interneuron_slope,
    )


def integrate(init_state, outside_afferent, coupling):

    def one_step(carry, applied_stimulus):
        fresh = advance(carry, applied_stimulus, outside_afferent)
        return (fresh, fresh[1] - fresh[2])

    begin = tuple((init_state[member] for member in range(6)))
    final, potentials = lax.scan(one_step, begin, coupling)
    return (jnp.stack(final), potentials)


def body(connectome, history, delays, cycle_head, outside_afferent, init_state, lead_field):
    tgt_rows = connectome.shape[0]
    target_blocks = delays.shape[0]
    source_blocks = delays.shape[1]
    block_rows = tgt_rows // target_blocks
    block_cols = connectome.shape[1] // source_blocks
    members = history.shape[1]
    slots_all = history.shape[0] * lax.axis_size("tgt")
    tiles = connectome.reshape(target_blocks, block_rows, source_blocks, block_cols)
    moments = jnp.arange(STEPS, dtype=jnp.int32)
    lag_slot = (cycle_head[0] + moments[None, None, :] - delays[:, :, None]) % slots_all
    whole = lax.all_gather(history, "tgt", axis=0, tiled=True)
    stacked = whole.reshape(slots_all, members, source_blocks, block_cols)
    slot_ids = jnp.arange(slots_all, dtype=jnp.int32)
    wanted = lag_slot[0].T
    picker = (wanted[:, None, :] == slot_ids[None, :, None]).astype(jnp.bfloat16)
    window = jnp.einsum(
        "tkb,kmbs->tmbs", picker, stacked, preferred_element_type=jnp.float32
    ).astype(jnp.bfloat16)
    pieces = jnp.einsum("rbs,tmbs->tmr", tiles[0], window, preferred_element_type=jnp.float32)
    share = tgt_rows // lax.axis_size("src")
    offset_rows = lax.axis_index("src") * share
    summed = lax.psum(pieces, "src")
    final_full, potentials = integrate(init_state, outside_afferent, summed)
    final_state = lax.dynamic_slice_in_dim(final_full, offset_rows, share, 2)
    potential = potentials.astype(jnp.bfloat16)
    signal = lax.psum_scatter(
        jnp.einsum("tmr,rs->mts", potential, lead_field, preferred_element_type=jnp.float32),
        "tgt",
        scatter_dimension=0,
        tiled=True,
    )
    return (signal, final_state)


def solution(mesh):
    in_specs = (
        P("tgt", "src"),
        P("tgt", None, "src"),
        P("tgt", "src"),
        P(),
        P(),
        P(None, None, "tgt"),
        P("tgt", None),
    )
    out_specs = (P("tgt", None, None), P(None, None, ("tgt", "src")))
    return jax.shard_map(body, mesh=mesh, in_specs=in_specs, out_specs=out_specs, check_vma=False)
```

profile of v0, /device:TPU:0, one launch (start us, length us, event | category | flops | bytes accessed | tf_op | source)
XLA Modules:
  0.0 964.4 jit_solution(11278450876451124406)
XLA Ops:
  7.2 0.0 copy-start
  7.2 0.0 all-gather.2.cloned.1.call-start
  7.2 0.7 all-gather.2.cloned.1.call-update
  7.9 0.0 reduce-scatter.2.cloned.1.call-start
  8.6 0.8 add_select_fusion
  9.4 0.2 fusion.14
  9.6 1.6 copy.13
  11.1 0.8 slice_bitcast_fusion
  11.9 538.7 %all-gather.2.cloned.1.call-done = bf16[32,32,51200]{2,1,0:T(8,128)(2,1)} async-done(((bf16[1,32,51200]{2,1,0:T(8,128)(2,1)}), bf16[32,32,51200]{2,1,0:T(8,128)(2,1)}) %all-gather.2.cloned.1.call-update) | async-done | bytes 104857616 | tf_op jit(solution)/shard_map/all_gather | solution.py:93
  550.7 67.9 %copy.18 = bf16[128,8,400,128]{3,2,1,0:T(8,128)(2,1)} copy(bf16[128,8,400,128]{3,1,2,0:T(8,128)(2,1)} %bitcast.26) | data formatting | bytes 209715200
  618.6 170.7 %fusion.5 = bf16[400,16,32,128]{3,1,2,0:T(8,128)(2,1)} fusion(pred[16,32,400,1]{1,0,3,2:T(8,128)(4,1)S(1)} %copy.13, bf16[32,32,400,128]{3,2,1,0:T(8,128)(2,1)} %bitcast.28), kind=kOutput, calls=%fused_computation.13 | convolution fusion | flops 1677721600 | bytes 157491200 | tf_op jit(solution)/shard_map/tkb,kmbs->tmbs/dot_general | solution.py:98
  789.3 0.0 copy-start.1
  789.3 32.4 %fusion.11 = f32[16,32,128]{2,1,0:T(8,128)S(1)} fusion(bf16[400,16,32,128]{3,1,2,0:T(8,128)(2,1)} %fusion.5, bf16[128,51200]{1,0:T(8,128)(2,1)} %param.9), kind=kOutput, calls=%fused_computation.20 | convolution fusion | flops 6710886400 | bytes 65798144 | tf_op jit(solution)/shard_map/rbs,tmbs->tmr/dot_general | solution.py:101
  821.7 0.0 copy-done.1
  821.7 2.1 while.25
  821.8 0.1 multiply_add_fusion.8
  821.9 0.1 multiply_add_fusion.8
  822.0 0.1 multiply_add_fusion.8
  822.2 0.1 multiply_add_fusion.8
  822.3 0.1 multiply_add_fusion.8
  822.4 0.1 multiply_add_fusion.8
  822.6 0.1 multiply_add_fusion.8
  822.7 0.1 multiply_add_fusion.8
  822.8 0.1 multiply_add_fusion.8
  823.0 0.1 multiply_add_fusion.8
  823.1 0.1 multiply_add_fusion.8
  823.2 0.1 multiply_add_fusion.8
  823.4 0.1 multiply_add_fusion.8
  823.5 0.1 multiply_add_fusion.8
  823.6 0.1 multiply_add_fusion.8
  823.8 0.1 multiply_add_fusion.8
  823.9 0.0 copy-done
  823.9 0.2 convolution_bitcast_fusion
  824.1 1.1 copy.12
  825.2 0.0 reduce-scatter.2.cloned.1.call-update
  825.3 0.0 copy-start.2
  825.3 132.3 %reduce-scatter.2.cloned.1.call-done = f32[1,16,256]{2,1,0:T(8,128)} async-done(((f32[32,16,256]{2,1,0:T(8,128)}), f32[1,16,256]{2,1,0:T(8,128)}) %reduce-scatter.2.cloned.1.call-update) | async-done | bytes 16400 | tf_op jit(solution)/shard_map/reduce_scatter | solution.py:108
  957.6 0.0 copy-done.2
  (56 shorter events, 0.4 us)
Async XLA Ops:
  7.2 816.7 %copy-start = (bf16[128,256]{1,0:T(8,128)(2,1)S(1)}, bf16[128,256]{1,0:T(8,128)(2,1)}, u32[]{:S(2)}) copy-start(bf16[128,256]{1,0:T(8,128)(2,1)} %param.15) | copy-start | bytes 196612
  7.2 543.5 %all-gather.2.cloned.1.call-start = ((), (), s32[]{:S(2)}) async-start(), calls=%async_computation.1 | async-start | bytes 108134400 | tf_op jit(solution)/shard_map/all_gather | solution.py:93
  7.9 949.7 %reduce-scatter.2.cloned.1.call-start = ((), (), s32[]{:S(2)}) async-start(), calls=%async_computation.2 | async-start | bytes 540672 | tf_op jit(solution)/shard_map/reduce_scatter | solution.py:108
  789.3 32.4 %copy-start.1 = (f32[32]{0:T(128)S(1)}, f32[32]{0:T(128)}, u32[]{:S(2)}) copy-start(f32[32]{0:T(128)} %param.13) | copy-start | bytes 388
  825.3 132.3 %copy-start.2 = (f32[6,32,128]{2,1,0:T(8,128)}, f32[6,32,128]{2,1,0:T(8,128)S(1)}, u32[]{:S(2)}) copy-start(f32[6,32,128]{2,1,0:T(8,128)S(1)} %bitcast_dynamic-update-slice_fusion.1) | copy-start | bytes 294916
Sparse Core Ops, SparseCore 0:
  10.8 539.8 all-gather.1
  825.4 132.1 reduce-scatter.1
where the time goes:
time: 965 us; the launch traced here: 964 us
  waiting for transfers between devices  672 us (70%)
  matrix products  203 us (21%)
  local copies, waits for them, and re-layouts  71.6 us (7%)
  between operations  14.8 us (2%)
    all_gather x1, waiting for transfers between devices, body(): whole = lax.all_gather(history, 'tgt', axis=0, tiled=True)  539 us
    dot_general x1, matrix products, body(): jnp.einsum('tkb,kmbs->tmbs', picker, stacked, preferred_element_type=jnp....  171 us
    reduce_scatter x1, waiting for transfers between devices, body(): lax.psum_scatter(jnp.einsum('tmr,rs->mts', potential, lead_field, preferr...  132 us
    unnamed x12, local copies, waits for them, and re-layouts  68 us
    dot_general x1, matrix products, body(): jnp.einsum('rbs,tmbs->tmr', tiles[0], window, preferred_element_type=jnp....  32.4 us
  transfers between devices with their start and end apart: 2, of which 2 were waited for; matrix products, arithmetic and copies ran while one was open for 0% of the time, Pallas kernels for 0%

commit v1 on v0

--- a/solution.py
+++ b/solution.py
@@ -1,9 +1,16 @@
+import functools
+
 import jax
 import jax.numpy as jnp
 from jax import lax
+from jax.experimental import pallas as pl
+from jax.experimental.pallas import tpu as pltpu
 from jax.sharding import PartitionSpec as P
 
 STEPS = 16
+MESH = pl.DeviceIdType.MESH
+GROUP = 8
+CHUNKS = 5
 
 
 integrator_step_width = 0.1
@@ -41,7 +48,7 @@
         - principal_cell_depolarization
     )
     summed_afferent_rate = (
-        outside_afferent[:, None]
+        outside_afferent
         + recurrent_loop_contacts
         * spike_rate_response(stellate_contact_count * principal_cell_depolarization)
         + global_link_scale * applied_stimulus
@@ -71,7 +78,7 @@
 def integrate(init_state, outside_afferent, coupling):
 
     def one_step(carry, applied_stimulus):
-        fresh = advance(carry, applied_stimulus, outside_afferent)
+        fresh = advance(carry, applied_stimulus, outside_afferent[:, None])
         return (fresh, fresh[1] - fresh[2])
 
     begin = tuple((init_state[member] for member in range(6)))
@@ -114,6 +121,436 @@
     return (signal, final_state)
 
 
+def fused_kernel(
+    planes,
+    conn_ref,
+    hist_ref,
+    delay_ref,
+    head_ref,
+    outside_ref,
+    init_ref,
+    lead_ref,
+    signal_ref,
+    final_ref,
+    *scratch,
+):
+    held = scratch[:CHUNKS]
+    tiles = scratch[CHUNKS : 2 * CHUNKS]
+    (
+        delay_vmem,
+        delay_smem,
+        acc,
+        parts,
+        pot,
+        eeg,
+        eeg_plane,
+        eeg_sum,
+        eeg_line,
+        piece_send,
+        piece_recv,
+        up_send,
+        up_recv,
+        down_send,
+        down_recv,
+        tile_send,
+        tile_recv,
+        delay_send,
+        delay_recv,
+        delay_local,
+        part_send,
+        part_recv,
+        plane_send,
+        plane_recv,
+        line_send,
+        line_recv,
+    ) = scratch[2 * CHUNKS :]
+    me = lax.axis_index("tgt")
+    z = me // GROUP
+    p = me % GROUP
+    rows = conn_ref.shape[0]
+    members = hist_ref.shape[1]
+    share = conn_ref.shape[1] // GROUP
+    width = share // CHUNKS
+    blocks = delay_ref.shape[1] // GROUP
+    chunk_blocks = blocks // CHUNKS
+    block_cols = width // chunk_blocks
+
+    def peer(off):
+        return lax.rem(p + off, GROUP)
+
+    def line(off):
+        return lax.rem(z + off, planes)
+
+    def device(plane, place):
+        return {"tgt": plane * GROUP + place}
+
+    barrier = pltpu.get_barrier_semaphore()
+    for off in range(1, GROUP):
+        pl.semaphore_signal(barrier, inc=1, device_id=device(z, peer(off)), device_id_type=MESH)
+    for off in range(1, planes):
+        pl.semaphore_signal(barrier, inc=1, device_id=device(line(off), p), device_id_type=MESH)
+    pl.semaphore_wait(barrier, GROUP + planes - 2)
+
+    def remote(src, dst, send, recv, plane, place):
+        return pltpu.make_async_remote_copy(
+            src_ref=src, dst_ref=dst, send_sem=send, recv_sem=recv,
+            device_id=device(plane, place), device_id_type=MESH,
+        )
+
+    def columns(place, c):
+        return pl.ds(pl.multiple_of(place * share + c * width, 128), width)
+
+    def piece_copy(c, off):
+        return remote(
+            hist_ref.at[0, :, columns(peer(off), c)], held[c].at[me],
+            piece_send.at[c, off], piece_recv.at[c, p], z, peer(off),
+        )
+
+    def own_piece(c):
+        return pltpu.make_async_copy(
+            hist_ref.at[0, :, columns(p, c)], held[c].at[me], piece_recv.at[c, p]
+        )
+
+    def piece_arrival(c, off):
+        slot = z * GROUP + peer(off)
+        return remote(
+            held[c].at[slot], held[c].at[slot],
+            piece_send.at[c, off], piece_recv.at[c, peer(off)], z, peer(off),
+        )
+
+    def tile_copy(c, off):
+        return remote(
+            conn_ref.at[:, columns(peer(off), c)], tiles[c].at[p],
+            tile_send.at[c, off], tile_recv.at[c, p], z, peer(off),
+        )
+
+    def own_tile(c):
+        return pltpu.make_async_copy(
+            conn_ref.at[:, columns(p, c)], tiles[c].at[p], tile_recv.at[c, p]
+        )
+
+    def tile_arrival(c, off):
+        return remote(
+            tiles[c].at[peer(off)], tiles[c].at[peer(off)],
+            tile_send.at[c, off], tile_recv.at[c, peer(off)], z, peer(off),
+        )
+
+    def delay_copy(off):
+        return remote(
+            delay_ref, delay_vmem.at[p], delay_send.at[off], delay_recv.at[p], z, peer(off)
+        )
+
+    def delay_arrival(off):
+        return remote(
+            delay_ref, delay_vmem.at[peer(off)],
+            delay_send.at[off], delay_recv.at[peer(off)], z, peer(off),
+        )
+
+    def plane_rows(plane):
+        return pl.ds(plane * GROUP, GROUP)
+
+    def up_copy(c, k):
+        span = held[c].at[plane_rows(z - k)]
+        return remote(span, span, up_send.at[c, k], up_recv.at[c, k], z + 1, p)
+
+    def up_arrival(c, k):
+        span = held[c].at[plane_rows(z - 1 - k)]
+        return remote(span, span, up_send.at[c, k], up_recv.at[c, k], z - 1, p)
+
+    def down_copy(c, k):
+        span = held[c].at[plane_rows(z + k)]
+        return remote(span, span, down_send.at[c, k], down_recv.at[c, k], z - 1, p)
+
+    def down_arrival(c, k):
+        span = held[c].at[plane_rows(z + 1 + k)]
+        return remote(span, span, down_send.at[c, k], down_recv.at[c, k], z + 1, p)
+
+    def sends_up(k):
+        return (z + 1 < planes) & (z - k >= 0)
+
+    def sends_down(k):
+        return (z - 1 >= 0) & (z + k < planes)
+
+    def send_pieces(c):
+        own_piece(c).start()
+        for off in range(1, GROUP):
+            piece_copy(c, off).start()
+
+    def send_tiles(c):
+        own_tile(c).start()
+        for off in range(1, GROUP):
+            tile_copy(c, off).start()
+
+    def forward(c, k):
+        @pl.when(sends_up(k))
+        def _():
+            up_copy(c, k).start()
+
+        @pl.when(sends_down(k))
+        def _():
+            down_copy(c, k).start()
+
+    def line_stage(c, k):
+        @pl.when(z - 1 - k >= 0)
+        def _():
+            up_arrival(c, k).wait_recv()
+
+        @pl.when(z + 1 + k < planes)
+        def _():
+            down_arrival(c, k).wait_recv()
+
+        if k + 2 < planes:
+            forward(c, k + 1)
+
+    def plane_stage(c):
+        own_piece(c).wait()
+        for off in range(1, GROUP):
+            piece_arrival(c, off).wait_recv()
+        forward(c, 0)
+
+    head = head_ref[0]
+
+    def product(c, a):
+        total = None
+        step = 2 if chunk_blocks % 2 == 0 else 1
+        for first in range(0, chunk_blocks, step):
+            spans = []
+            for b in range(first, first + step):
+                base = head + 2 * planes * GROUP - delay_smem[a, 0, p * blocks + c * chunk_blocks + b]
+                spans.append(
+                    jnp.concatenate(
+                        [
+                            held[c][
+                                lax.rem(base + t, planes * GROUP),
+                                :,
+                                b * block_cols : (b + 1) * block_cols,
+                            ]
+                            for t in range(STEPS)
+                        ],
+                        axis=0,
+                    )
+                )
+            window = jnp.concatenate(spans, axis=1)
+            term = lax.dot_general(
+                window,
+                tiles[c][a, :, first * block_cols : (first + step) * block_cols],
+                (((1,), (1,)), ((), ())),
+                preferred_element_type=jnp.float32,
+            )
+            total = term if total is None else total + term
+        return total
+
+    def part_copy(off):
+        return remote(
+            acc.at[peer(off)], parts.at[p], part_send.at[off], part_recv.at[p], z, peer(off)
+        )
+
+    def part_arrival(off):
+        return remote(
+            acc.at[peer(off)], parts.at[peer(off)],
+            part_send.at[off], part_recv.at[peer(off)], z, peer(off),
+        )
+
+    def compute(c):
+        own_tile(c).wait()
+        for off in range(1, GROUP):
+            tile_arrival(c, off).wait_recv()
+
+        def one(off, carry):
+            a = lax.rem(p + 1 + off, GROUP)
+            if c == 0:
+                acc[a] = product(c, a)
+            else:
+                acc[a] += product(c, a)
+            return carry
+
+        if c < CHUNKS - 1:
+            lax.fori_loop(0, GROUP, one, 0)
+        else:
+            for off in range(GROUP):
+                one(off, 0)
+                if off < GROUP - 1:
+                    part_copy(off + 1).start()
+
+    for off in range(1, GROUP):
+        delay_copy(off).start()
+    own_delay = pltpu.make_async_copy(delay_ref, delay_vmem.at[p], delay_recv.at[p])
+    own_delay.start()
+    send_pieces(0)
+    send_pieces(1)
+    for s in range(CHUNKS + planes - 1):
+        if s < CHUNKS:
+            plane_stage(s)
+            send_tiles(s)
+            if s + 2 < CHUNKS:
+                send_pieces(s + 2)
+        if s == 0:
+            own_delay.wait()
+            for off in range(1, GROUP):
+                delay_arrival(off).wait_recv()
+            table = pltpu.make_async_copy(delay_vmem, delay_smem, delay_local)
+            table.start()
+            table.wait()
+        for k in range(planes - 1):
+            if 0 <= s - 1 - k < CHUNKS:
+                line_stage(s - 1 - k, k)
+        if 0 <= s - planes + 1 < CHUNKS:
+            compute(s - planes + 1)
+
+    parts[p] = acc[p]
+    for off in range(1, GROUP):
+        part_arrival(off).wait_recv()
+
+    state = tuple(init_ref[i] for i in range(6))
+    outside = outside_ref[...]
+    for t in range(STEPS):
+        stimulus = parts[0, t * members : (t + 1) * members, :]
+        for q in range(1, GROUP):
+            stimulus = stimulus + parts[q, t * members : (t + 1) * members, :]
+        state = advance(state, stimulus, outside)
+        pot[t * members : (t + 1) * members, :] = (state[1] - state[2]).astype(jnp.bfloat16)
+    for i in range(6):
+        final_ref[i] = state[i]
+
+    count = STEPS * members
+    row = lax.broadcasted_iota(jnp.int32, (count, count), 0)
+    col = lax.broadcasted_iota(jnp.int32, (count, count), 1)
+    order = jnp.where(col == (row % STEPS) * members + row // STEPS, 1.0, 0.0).astype(jnp.bfloat16)
+    ordered = jnp.dot(order, pot[...], preferred_element_type=jnp.float32).astype(jnp.bfloat16)
+    sensors = lead_ref.shape[1]
+    eeg[...] = jnp.dot(ordered, lead_ref[...], preferred_element_type=jnp.float32).reshape(
+        planes, GROUP, STEPS, sensors
+    )
+
+    def plane_copy(off):
+        return remote(
+            eeg.at[:, peer(off)], eeg_plane.at[p], plane_send.at[off], plane_recv.at[p], z, peer(off)
+        )
+
+    def plane_arrival(off):
+        return remote(
+            eeg.at[:, peer(off)], eeg_plane.at[peer(off)],
+            plane_send.at[off], plane_recv.at[peer(off)], z, peer(off),
+        )
+
+    for off in range(1, GROUP):
+        plane_copy(off).start()
+    eeg_plane[p] = eeg[:, p]
+    for off in range(1, GROUP):
+        plane_arrival(off).wait_recv()
+    over_plane = eeg_plane[0]
+    for q in range(1, GROUP):
+        over_plane = over_plane + eeg_plane[q]
+    eeg_sum[...] = over_plane
+
+    def line_copy(off):
+        return remote(
+            eeg_sum.at[line(off)], eeg_line.at[z], line_send.at[off], line_recv.at[z], line(off), p
+        )
+
+    def line_arrival(off):
+        return remote(
+            eeg_sum.at[line(off)], eeg_line.at[line(off)],
+            line_send.at[off], line_recv.at[line(off)], line(off), p,
+        )
+
+    for off in range(1, planes):
+        line_copy(off).start()
+    eeg_line[z] = eeg_sum[z]
+    for off in range(1, planes):
+        line_arrival(off).wait_recv()
+    over_line = eeg_line[0]
+    for q in range(1, planes):
+        over_line = over_line + eeg_line[q]
+    signal_ref[0] = over_line
+
+    for off in range(1, GROUP):
+        delay_copy(off).wait_send()
+        part_copy(off).wait_send()
+        plane_copy(off).wait_send()
+    for off in range(1, planes):
+        line_copy(off).wait_send()
+    for c in range(CHUNKS):
+        for off in range(1, GROUP):
+            piece_copy(c, off).wait_send()
+            tile_copy(c, off).wait_send()
+        for k in range(planes - 1):
+            @pl.when(sends_up(k))
+            def _(c=c, k=k):
+                up_copy(c, k).wait_send()
+
+            @pl.when(sends_down(k))
+            def _(c=c, k=k):
+                down_copy(c, k).wait_send()
+
+
+def fused_body(planes, connectome, history, delays, cycle_head, outside_afferent, init_state, lead_field):
+    rows, sources = connectome.shape
+    members = history.shape[1]
+    sensors = lead_field.shape[1]
+    slots = planes * GROUP
+    share = sources // GROUP
+    width = share // CHUNKS
+    count = STEPS * members
+    dma = pltpu.SemaphoreType.DMA
+    f32 = jnp.float32
+    vmem = pl.BlockSpec(memory_space=pltpu.VMEM)
+    hbm = pl.BlockSpec(memory_space=pl.ANY)
+    return pl.pallas_call(
+        functools.partial(fused_kernel, planes),
+        out_shape=(
+            jax.ShapeDtypeStruct((1, STEPS, sensors), f32),
+            jax.ShapeDtypeStruct(init_state.shape, f32),
+        ),
+        in_specs=[hbm, hbm, hbm, pl.BlockSpec(memory_space=pltpu.SMEM), vmem, vmem, vmem],
+        out_specs=(vmem, vmem),
+        scratch_shapes=[pltpu.VMEM((slots, members, width), jnp.bfloat16) for _ in range(CHUNKS)]
+        + [pltpu.VMEM((GROUP, rows, width), jnp.bfloat16) for _ in range(CHUNKS)]
+        + [
+            pltpu.VMEM((GROUP, 1, delays.shape[1]), jnp.int32),
+            pltpu.SMEM((GROUP, 1, delays.shape[1]), jnp.int32),
+            pltpu.VMEM((GROUP, count, rows), f32),
+            pltpu.VMEM((GROUP, count, rows), f32),
+            pltpu.VMEM((count, rows), jnp.bfloat16),
+            pltpu.VMEM((planes, GROUP, STEPS, sensors), f32),
+            pltpu.VMEM((GROUP, planes, STEPS, sensors), f32),
+            pltpu.VMEM((planes, STEPS, sensors), f32),
+            pltpu.VMEM((planes, STEPS, sensors), f32),
+            dma((CHUNKS, GROUP)),
+            dma((CHUNKS, GROUP)),
+            dma((CHUNKS, planes)),
+            dma((CHUNKS, planes)),
+            dma((CHUNKS, planes)),
+            dma((CHUNKS, planes)),
+            dma((CHUNKS, GROUP)),
+            dma((CHUNKS, GROUP)),
+            dma((GROUP,)),
+            dma((GROUP,)),
+            dma,
+            dma((GROUP,)),
+            dma((GROUP,)),
+            dma((GROUP,)),
+            dma((GROUP,)),
+            dma((planes,)),
+            dma((planes,)),
+        ],
+        compiler_params=pltpu.CompilerParams(
+            collective_id=0, has_side_effects=True, vmem_limit_bytes=56 * 1024 * 1024
+        ),
+        cost_estimate=pl.CostEstimate(
+            flops=2 * rows * sources * count, bytes_accessed=4 * rows * sources, transcendentals=0
+        ),
+    )(
+        connectome,
+        history,
+        delays,
+        cycle_head,
+        jnp.broadcast_to(outside_afferent[:, None], (members, rows)),
+        init_state,
+        lead_field,
+    )
+
+
 def solution(mesh):
     in_specs = (
         P("tgt", "src"),
@@ -125,4 +562,8 @@
         P("tgt", None),
     )
     out_specs = (P("tgt", None, None), P(None, None, ("tgt", "src")))
-    return jax.shard_map(body, mesh=mesh, in_specs=in_specs, out_specs=out_specs, check_vma=False)
+    devices = mesh.shape["tgt"]
+    chosen = body
+    if mesh.shape["src"] == 1 and devices % GROUP == 0 and devices > GROUP:
+        chosen = functools.partial(fused_body, devices // GROUP)
+    return jax.shard_map(chosen, mesh=mesh, in_specs=in_specs, out_specs=out_specs, check_vma=False)

time: 965 us -> 273 us (0.28)
  waiting for transfers between devices: 672 us -> 0 us
  Pallas kernels: 0 us -> 267 us
  matrix products: 203 us -> 0 us
  local copies, waits for them, and re-layouts: 71.6 us -> 4.19 us
  between operations: 14.8 us -> 1.29 us
    all_gather x1 -> x0, waiting for transfers between devices: 539 us -> none  [body(): whole = lax.all_gather(history, 'tgt', axis=0, tiled=True)]
    pallas_call x0 -> x1, Pallas kernels: none -> 267 us  [fused_body(): pl.pallas_call(functools.partial(fused_kernel, planes), out_shape=(jax.Sh...]
    dot_general x3 -> x0, matrix products: 203 us -> none  [the longest x1 171 us: body(): jnp.einsum('tkb,kmbs->tmbs', picker, stacked, preferred_element_type=jnp....]
    reduce_scatter x1 -> x0, waiting for transfers between devices: 132 us -> none  [body(): lax.psum_scatter(jnp.einsum('tmr,rs->mts', potential, lead_field, preferr...]
    unnamed x12 -> x2, local copies, waits for them, and re-layouts: 68 us -> 2.86 us
  transfers between devices with their start and end apart: 2 -> 0, of which waited for: 2 -> 0; matrix products, arithmetic and copies ran while one was open for 0% -> 0% of each run, Pallas kernels for 0% -> 0%
where the time goes in v1:
time: 273 us; the launch traced here: 272 us
  Pallas kernels  267 us (98%)
  local copies, waits for them, and re-layouts  4.19 us (2%)
    pallas_call x1, Pallas kernels, fused_body(): pl.pallas_call(functools.partial(fused_kernel, planes), out_shape=(jax.Sh...  267 us

profile of v1, /device:TPU:0, one launch (start us, length us, event | category | flops | bytes accessed | tf_op | source)
XLA Modules:
  0.0 272.2 jit_solution(14077593685348875222)
XLA Ops:
  1.3 1.3 broadcast_in_dim.2.outside_ref
  2.6 266.8 %shard_map.86 = (f32[1,16,256]{2,1,0:T(8,128)}, f32[6,32,128]{2,1,0:T(8,128)}) custom-call(bf16[128,51200]{1,0:T(8,128)(2,1)} %conn_ref.1, bf16[1,32,51200]{2,1,0:T(8,128)(2,1)} %hist_ref.1, s32[1,400]{1,0:T(1,128)} %delay_ref.1, s32[1]{0:T(128)S(6)} %copy.11.head_ref, f32[32,128]{1,0:T(8,128)} %broadcast_in_dim.2.outside_ref, f32[6,32,128]{2,1,0:T(8,128)} %init_ref.1, ...), custom_call_target="tpu_custom_call" | custom-call | flops 6710886400 | bytes 26214400 | tf_op jit(solution)/shard_map/pallas_call | solution.py:499
  269.4 1.3 copy.12
  270.7 1.5 copy.13

commit v2 on v1

--- a/solution.py
+++ b/solution.py
@@ -10,7 +10,13 @@
 STEPS = 16
 MESH = pl.DeviceIdType.MESH
 GROUP = 8
-CHUNKS = 5
+CHIPS = GROUP // 2
+CUTS = (0.28, 0.48, 0.68, 0.88, 1.0)
+CHUNKS = len(CUTS)
+
+
+def chunk_starts(blocks):
+    return [0] + [2 * round(cut * blocks / 2) for cut in CUTS[:-1]] + [blocks]
 
 
 integrator_step_width = 0.1
@@ -139,8 +145,18 @@
     (
         delay_vmem,
         delay_smem,
+        other_delay_vmem,
+        other_delay_smem,
+        other_tiles,
         acc,
+        pair,
         parts,
+        other_acc,
+        other_pair,
+        other_parts,
+        handed,
+        returned,
+        coupling,
         pot,
         eeg,
         eeg_plane,
@@ -157,8 +173,20 @@
         delay_send,
         delay_recv,
         delay_local,
+        pair_send,
+        pair_recv,
         part_send,
         part_recv,
+        other_pair_send,
+        other_pair_recv,
+        other_part_send,
+        other_part_recv,
+        other_tile_send,
+        other_tile_recv,
+        other_delay_send,
+        other_delay_recv,
+        return_send,
+        return_recv,
         plane_send,
         plane_recv,
         line_send,
@@ -167,13 +195,19 @@
     me = lax.axis_index("tgt")
     z = me // GROUP
     p = me % GROUP
+    core = p % 2
+    chip = p // 2
+    is_end = (z == 0) | (z == planes - 1)
+    is_inner = (z > 0) & (z < planes - 1)
+    serves = (z == 1) | (z == planes - 2)
+    inward = jnp.where(z == 0, 1, planes - 2)
+    outward = jnp.where(z == 1, 0, planes - 1)
     rows = conn_ref.shape[0]
     members = hist_ref.shape[1]
     share = conn_ref.shape[1] // GROUP
-    width = share // CHUNKS
     blocks = delay_ref.shape[1] // GROUP
-    chunk_blocks = blocks // CHUNKS
-    block_cols = width // chunk_blocks
+    block_cols = share // blocks
+    starts = chunk_starts(blocks)
 
     def peer(off):
         return lax.rem(p + off, GROUP)
@@ -198,7 +232,8 @@
         )
 
     def columns(place, c):
-        return pl.ds(pl.multiple_of(place * share + c * width, 128), width)
+        width = (starts[c + 1] - starts[c]) * block_cols
+        return pl.ds(pl.multiple_of(place * share + starts[c] * block_cols, 128), width)
 
     def piece_copy(c, off):
         return remote(
@@ -265,11 +300,14 @@
         span = held[c].at[plane_rows(z + 1 + k)]
         return remote(span, span, down_send.at[c, k], down_recv.at[c, k], z + 1, p)
 
-    def sends_up(k):
-        return (z + 1 < planes) & (z - k >= 0)
-
-    def sends_down(k):
-        return (z - 1 >= 0) & (z + k < planes)
+    def edge(c):
+        return 1 if c == 0 else 0
+
+    def sends_up(c, k):
+        return (z + 1 < planes - edge(c)) & (z - k >= 0)
+
+    def sends_down(c, k):
+        return (z - 1 >= edge(c)) & (z + k < planes)
 
     def send_pieces(c):
         own_piece(c).start()
@@ -282,20 +320,20 @@
             tile_copy(c, off).start()
 
     def forward(c, k):
-        @pl.when(sends_up(k))
+        @pl.when(sends_up(c, k))
         def _():
             up_copy(c, k).start()
 
-        @pl.when(sends_down(k))
+        @pl.when(sends_down(c, k))
         def _():
             down_copy(c, k).start()
 
     def line_stage(c, k):
-        @pl.when(z - 1 - k >= 0)
+        @pl.when((z - 1 - k >= 0) & (z < planes - edge(c)))
         def _():
             up_arrival(c, k).wait_recv()
 
-        @pl.when(z + 1 + k < planes)
+        @pl.when((z + 1 + k < planes) & (z >= edge(c)))
         def _():
             down_arrival(c, k).wait_recv()
 
@@ -310,13 +348,14 @@
 
     head = head_ref[0]
 
-    def product(c, a):
+    def product(c, a, tile, table):
         total = None
-        step = 2 if chunk_blocks % 2 == 0 else 1
-        for first in range(0, chunk_blocks, step):
+        count = starts[c + 1] - starts[c]
+        for first in range(0, count, 2):
+            last = min(first + 2, count)
             spans = []
-            for b in range(first, first + step):
-                base = head + 2 * planes * GROUP - delay_smem[a, 0, p * blocks + c * chunk_blocks + b]
+            for b in range(first, last):
+                base = head + 2 * planes * GROUP - table[a, 0, p * blocks + starts[c] + b]
                 spans.append(
                     jnp.concatenate(
                         [
@@ -333,57 +372,154 @@
             window = jnp.concatenate(spans, axis=1)
             term = lax.dot_general(
                 window,
-                tiles[c][a, :, first * block_cols : (first + step) * block_cols],
+                tile[a, :, first * block_cols : last * block_cols],
                 (((1,), (1,)), ((), ())),
                 preferred_element_type=jnp.float32,
             )
             total = term if total is None else total + term
         return total
 
-    def part_copy(off):
-        return remote(
-            acc.at[peer(off)], parts.at[p], part_send.at[off], part_recv.at[p], z, peer(off)
-        )
-
-    def part_arrival(off):
-        return remote(
-            acc.at[peer(off)], parts.at[peer(off)],
-            part_send.at[off], part_recv.at[peer(off)], z, peer(off),
-        )
-
-    def compute(c):
+    class Sum:
+        def __init__(self, own, pair, parts, pair_send, pair_recv, part_send, part_recv):
+            self.own, self.pair, self.parts = own, pair, parts
+            self.pair_send, self.pair_recv = pair_send, pair_recv
+            self.part_send, self.part_recv = part_send, part_recv
+
+        def pair_copy(self, j):
+            return remote(
+                self.own.at[2 * j + 1 - core], self.pair.at[j],
+                self.pair_send.at[j], self.pair_recv.at[j], z, 2 * chip + 1 - core,
+            )
+
+        def part_copy(self, off):
+            j = lax.rem(chip + off, CHIPS)
+            return remote(
+                self.own.at[2 * j + core], self.parts.at[chip],
+                self.part_send.at[off], self.part_recv.at[chip], z, 2 * j + core,
+            )
+
+        def part_arrival(self, off):
+            j = lax.rem(chip + off, CHIPS)
+            return remote(
+                self.own.at[2 * j + core], self.parts.at[j],
+                self.part_send.at[off], self.part_recv.at[j], z, 2 * j + core,
+            )
+
+        def pass_on(self, off):
+            j = lax.rem(chip + off, CHIPS)
+            self.pair_copy(j).wait_recv()
+            self.own[2 * j + core] += self.pair[j]
+            if off > 0:
+                self.part_copy(off).start()
+
+        def send(self, fill):
+            order = list(range(1, CHIPS)) + [0]
+            for at, off in enumerate(order):
+                j = lax.rem(chip + off, CHIPS)
+                fill(2 * j + 1 - core)
+                self.pair_copy(j).start()
+                fill(2 * j + core)
+                if at > 0:
+                    self.pass_on(order[at - 1])
+            self.pass_on(order[-1])
+
+        def total(self):
+            value = self.own[2 * chip + core]
+            for off in range(1, CHIPS):
+                self.part_arrival(off).wait_recv()
+                value = value + self.parts[lax.rem(chip + off, CHIPS)]
+            return value
+
+        def finish(self):
+            for j in range(CHIPS):
+                self.pair_copy(j).wait_send()
+            for off in range(1, CHIPS):
+                self.part_copy(off).wait_send()
+
+    main = Sum(acc, pair, parts, pair_send, pair_recv, part_send, part_recv)
+    other = Sum(
+        other_acc, other_pair, other_parts,
+        other_pair_send, other_pair_recv, other_part_send, other_part_recv,
+    )
+
+    def tiles_arrive(c):
         own_tile(c).wait()
         for off in range(1, GROUP):
             tile_arrival(c, off).wait_recv()
 
-        def one(off, carry):
-            a = lax.rem(p + 1 + off, GROUP)
-            if c == 0:
-                acc[a] = product(c, a)
-            else:
-                acc[a] += product(c, a)
-            return carry
+    def compute(c):
+        tiles_arrive(c)
+
+        def one(a):
+            acc[a] += product(c, a, tiles[c], delay_smem)
 
         if c < CHUNKS - 1:
-            lax.fori_loop(0, GROUP, one, 0)
+            lax.fori_loop(0, GROUP, lambda a, carry: (one(a), carry)[1], 0)
         else:
-            for off in range(GROUP):
-                one(off, 0)
-                if off < GROUP - 1:
-                    part_copy(off + 1).start()
+            main.send(one)
+
+    def other_tile_copy(a, plane):
+        return remote(
+            tiles[0].at[a], other_tiles.at[a], other_tile_send.at[a], other_tile_recv.at[a], plane, p
+        )
+
+    def other_delay_copy(plane):
+        return remote(
+            delay_vmem, other_delay_vmem, other_delay_send, other_delay_recv, plane, p
+        )
+
+    def hand_over():
+        other_delay_copy(inward).start()
+        own_tile(0).wait()
+        other_tile_copy(p, inward).start()
+        for off in range(1, GROUP):
+            tile_arrival(0, off).wait_recv()
+            other_tile_copy(peer(off), inward).start()
+
+    def compute_other():
+        other_delay_copy(outward).wait_recv()
+        table = pltpu.make_async_copy(other_delay_vmem, other_delay_smem, delay_local)
+        table.start()
+        table.wait()
+        for a in range(GROUP):
+            other_tile_copy(a, outward).wait_recv()
+
+        def one(a):
+            other_acc[a] = product(0, a, other_tiles, other_delay_smem)
+
+        other.send(one)
+
+    def return_copy(plane):
+        return remote(handed, returned, return_send, return_recv, plane, p)
+
+    def return_other():
+        handed[...] = other.total()
+        return_copy(outward).start()
 
     for off in range(1, GROUP):
         delay_copy(off).start()
     own_delay = pltpu.make_async_copy(delay_ref, delay_vmem.at[p], delay_recv.at[p])
     own_delay.start()
     send_pieces(0)
+
+    @pl.when(is_end)
+    def _():
+        send_tiles(0)
+
     send_pieces(1)
+
+    @pl.when(is_inner)
+    def _():
+        send_tiles(0)
+
+    acc[...] = jnp.zeros_like(acc)
     for s in range(CHUNKS + planes - 1):
         if s < CHUNKS:
             plane_stage(s)
-            send_tiles(s)
             if s + 2 < CHUNKS:
                 send_pieces(s + 2)
+            if s + 1 < CHUNKS:
+                send_tiles(s + 1)
         if s == 0:
             own_delay.wait()
             for off in range(1, GROUP):
@@ -391,22 +527,34 @@
             table = pltpu.make_async_copy(delay_vmem, delay_smem, delay_local)
             table.start()
             table.wait()
+            pl.when(is_end)(hand_over)
         for k in range(planes - 1):
             if 0 <= s - 1 - k < CHUNKS:
                 line_stage(s - 1 - k, k)
-        if 0 <= s - planes + 1 < CHUNKS:
-            compute(s - planes + 1)
-
-    parts[p] = acc[p]
-    for off in range(1, GROUP):
-        part_arrival(off).wait_recv()
+        if s == planes + 2:
+            pl.when(serves)(return_other)
+        c = s - planes + 1
+        if c == 0:
+            pl.when(is_inner)(functools.partial(compute, 0))
+        elif 0 < c < CHUNKS:
+            compute(c)
+        if s == planes:
+            pl.when(serves)(compute_other)
+
+    coupling[...] = main.total()
+
+    @pl.when(is_end)
+    def _():
+        return_copy(inward).wait_recv()
+        coupling[...] += returned[...]
 
     state = tuple(init_ref[i] for i in range(6))
-    outside = outside_ref[...]
+    member = lax.broadcasted_iota(jnp.int32, (members, rows), 0)
+    outside = jnp.zeros((members, rows), jnp.float32)
+    for m in range(members):
+        outside = jnp.where(member == m, outside_ref[m], outside)
     for t in range(STEPS):
-        stimulus = parts[0, t * members : (t + 1) * members, :]
-        for q in range(1, GROUP):
-            stimulus = stimulus + parts[q, t * members : (t + 1) * members, :]
+        stimulus = coupling[t * members : (t + 1) * members, :]
         state = advance(state, stimulus, outside)
         pot[t * members : (t + 1) * members, :] = (state[1] - state[2]).astype(jnp.bfloat16)
     for i in range(6):
@@ -466,8 +614,20 @@
 
     for off in range(1, GROUP):
         delay_copy(off).wait_send()
-        part_copy(off).wait_send()
         plane_copy(off).wait_send()
+    main.finish()
+
+    @pl.when(is_end)
+    def _():
+        other_delay_copy(inward).wait_send()
+        for a in range(GROUP):
+            other_tile_copy(a, inward).wait_send()
+
+    @pl.when(serves)
+    def _():
+        other.finish()
+        return_copy(outward).wait_send()
+
     for off in range(1, planes):
         line_copy(off).wait_send()
     for c in range(CHUNKS):
@@ -475,11 +635,11 @@
             piece_copy(c, off).wait_send()
             tile_copy(c, off).wait_send()
         for k in range(planes - 1):
-            @pl.when(sends_up(k))
+            @pl.when(sends_up(c, k))
             def _(c=c, k=k):
                 up_copy(c, k).wait_send()
 
-            @pl.when(sends_down(k))
+            @pl.when(sends_down(c, k))
             def _(c=c, k=k):
                 down_copy(c, k).wait_send()
 
@@ -490,11 +650,14 @@
     sensors = lead_field.shape[1]
     slots = planes * GROUP
     share = sources // GROUP
-    width = share // CHUNKS
+    blocks = delays.shape[1] // GROUP
+    starts = chunk_starts(blocks)
+    widths = [(stop - start) * (share // blocks) for start, stop in zip(starts, starts[1:])]
     count = STEPS * members
     dma = pltpu.SemaphoreType.DMA
     f32 = jnp.float32
     vmem = pl.BlockSpec(memory_space=pltpu.VMEM)
+    smem = pl.BlockSpec(memory_space=pltpu.SMEM)
     hbm = pl.BlockSpec(memory_space=pl.ANY)
     return pl.pallas_call(
         functools.partial(fused_kernel, planes),
@@ -502,15 +665,25 @@
             jax.ShapeDtypeStruct((1, STEPS, sensors), f32),
             jax.ShapeDtypeStruct(init_state.shape, f32),
         ),
-        in_specs=[hbm, hbm, hbm, pl.BlockSpec(memory_space=pltpu.SMEM), vmem, vmem, vmem],
+        in_specs=[hbm, hbm, hbm, smem, smem, vmem, vmem],
         out_specs=(vmem, vmem),
-        scratch_shapes=[pltpu.VMEM((slots, members, width), jnp.bfloat16) for _ in range(CHUNKS)]
-        + [pltpu.VMEM((GROUP, rows, width), jnp.bfloat16) for _ in range(CHUNKS)]
+        scratch_shapes=[pltpu.VMEM((slots, members, width), jnp.bfloat16) for width in widths]
+        + [pltpu.VMEM((GROUP, rows, width), jnp.bfloat16) for width in widths]
         + [
             pltpu.VMEM((GROUP, 1, delays.shape[1]), jnp.int32),
             pltpu.SMEM((GROUP, 1, delays.shape[1]), jnp.int32),
+            pltpu.VMEM((GROUP, 1, delays.shape[1]), jnp.int32),
+            pltpu.SMEM((GROUP, 1, delays.shape[1]), jnp.int32),
+            pltpu.VMEM((GROUP, rows, widths[0]), jnp.bfloat16),
             pltpu.VMEM((GROUP, count, rows), f32),
+            pltpu.VMEM((CHIPS, count, rows), f32),
+            pltpu.VMEM((CHIPS, count, rows), f32),
             pltpu.VMEM((GROUP, count, rows), f32),
+            pltpu.VMEM((CHIPS, count, rows), f32),
+            pltpu.VMEM((CHIPS, count, rows), f32),
+            pltpu.VMEM((count, rows), f32),
+            pltpu.VMEM((count, rows), f32),
+            pltpu.VMEM((count, rows), f32),
             pltpu.VMEM((count, rows), jnp.bfloat16),
             pltpu.VMEM((planes, GROUP, STEPS, sensors), f32),
             pltpu.VMEM((GROUP, planes, STEPS, sensors), f32),
@@ -527,8 +700,20 @@
             dma((GROUP,)),
             dma((GROUP,)),
             dma,
+            dma((CHIPS,)),
+            dma((CHIPS,)),
+            dma((CHIPS,)),
+            dma((CHIPS,)),
+            dma((CHIPS,)),
+            dma((CHIPS,)),
+            dma((CHIPS,)),
+            dma((CHIPS,)),
             dma((GROUP,)),
             dma((GROUP,)),
+            dma,
+            dma,
+            dma,
+            dma,
             dma((GROUP,)),
             dma((GROUP,)),
             dma((planes,)),
@@ -545,7 +730,7 @@
         history,
         delays,
         cycle_head,
-        jnp.broadcast_to(outside_afferent[:, None], (members, rows)),
+        outside_afferent,
         init_state,
         lead_field,
     )
@@ -564,6 +749,6 @@
     out_specs = (P("tgt", None, None), P(None, None, ("tgt", "src")))
     devices = mesh.shape["tgt"]
     chosen = body
-    if mesh.shape["src"] == 1 and devices % GROUP == 0 and devices > GROUP:
+    if mesh.shape["src"] == 1 and devices % GROUP == 0 and devices >= 4 * GROUP:
         chosen = functools.partial(fused_body, devices // GROUP)
     return jax.shard_map(chosen, mesh=mesh, in_specs=in_specs, out_specs=out_specs, check_vma=False)

time: 273 us -> 288 us (1.055)
  Pallas kernels: 267 us -> 284 us
    pallas_call x1, Pallas kernels: 267 us -> 284 us  [fused_body(): pl.pallas_call(functools.partial(fused_kernel, planes), out_shape=(jax.Sh...]
where the time goes in v2:
time: 288 us
  Pallas kernels  284 us (99%)
    pallas_call x1, Pallas kernels, fused_body(): pl.pallas_call(functools.partial(fused_kernel, planes), out_shape=(jax.Sh...  284 us

profile of v2, /device:TPU:0, one launch (start us, length us, event | category | flops | bytes accessed | tf_op | source)
XLA Modules:
  0.0 288.0 jit_solution(13354347297712460918)
XLA Ops:
  1.3 283.9 %shard_map.86 = (f32[1,16,256]{2,1,0:T(8,128)}, f32[6,32,128]{2,1,0:T(8,128)}) custom-call(bf16[128,51200]{1,0:T(8,128)(2,1)} %conn_ref.1, bf16[1,32,51200]{2,1,0:T(8,128)(2,1)} %hist_ref.1, s32[1,400]{1,0:T(1,128)} %delay_ref.1, s32[1]{0:T(128)S(6)} %copy.11.head_ref, f32[32]{0:T(128)} %outside_ref.1, f32[6,32,128]{2,1,0:T(8,128)} %init_ref.1, ...), custom_call_target="tpu_custom_call" | custom-call | flops 6710886400 | bytes 26214400 | tf_op jit(solution)/shard_map/pallas_call | solution.py:662
  285.1 1.3 copy.12
  286.5 1.5 copy.13

commit v3 on v2

--- a/solution.py
+++ b/solution.py
@@ -11,7 +11,7 @@
 MESH = pl.DeviceIdType.MESH
 GROUP = 8
 CHIPS = GROUP // 2
-CUTS = (0.28, 0.48, 0.68, 0.88, 1.0)
+CUTS = (0.2, 0.44, 0.68, 0.88, 1.0)
 CHUNKS = len(CUTS)
 
 
@@ -145,17 +145,9 @@
     (
         delay_vmem,
         delay_smem,
-        other_delay_vmem,
-        other_delay_smem,
-        other_tiles,
         acc,
         pair,
         parts,
-        other_acc,
-        other_pair,
-        other_parts,
-        handed,
-        returned,
         coupling,
         pot,
         eeg,
@@ -177,16 +169,6 @@
         pair_recv,
         part_send,
         part_recv,
-        other_pair_send,
-        other_pair_recv,
-        other_part_send,
-        other_part_recv,
-        other_tile_send,
-        other_tile_recv,
-        other_delay_send,
-        other_delay_recv,
-        return_send,
-        return_recv,
         plane_send,
         plane_recv,
         line_send,
@@ -199,9 +181,6 @@
     chip = p // 2
     is_end = (z == 0) | (z == planes - 1)
     is_inner = (z > 0) & (z < planes - 1)
-    serves = (z == 1) | (z == planes - 2)
-    inward = jnp.where(z == 0, 1, planes - 2)
-    outward = jnp.where(z == 1, 0, planes - 1)
     rows = conn_ref.shape[0]
     members = hist_ref.shape[1]
     share = conn_ref.shape[1] // GROUP
@@ -300,14 +279,11 @@
         span = held[c].at[plane_rows(z + 1 + k)]
         return remote(span, span, down_send.at[c, k], down_recv.at[c, k], z + 1, p)
 
-    def edge(c):
-        return 1 if c == 0 else 0
-
-    def sends_up(c, k):
-        return (z + 1 < planes - edge(c)) & (z - k >= 0)
-
-    def sends_down(c, k):
-        return (z - 1 >= edge(c)) & (z + k < planes)
+    def sends_up(k):
+        return (z + 1 < planes) & (z - k >= 0)
+
+    def sends_down(k):
+        return (z - 1 >= 0) & (z + k < planes)
 
     def send_pieces(c):
         own_piece(c).start()
@@ -320,23 +296,25 @@
             tile_copy(c, off).start()
 
     def forward(c, k):
-        @pl.when(sends_up(c, k))
+        @pl.when(sends_up(k))
         def _():
             up_copy(c, k).start()
 
-        @pl.when(sends_down(c, k))
+        @pl.when(sends_down(k))
         def _():
             down_copy(c, k).start()
 
-    def line_stage(c, k):
-        @pl.when((z - 1 - k >= 0) & (z < planes - edge(c)))
+    def line_arrives(c, k, here):
+        @pl.when((z - 1 - k >= 0) & here)
         def _():
             up_arrival(c, k).wait_recv()
 
-        @pl.when((z + 1 + k < planes) & (z >= edge(c)))
+        @pl.when((z + 1 + k < planes) & here)
         def _():
             down_arrival(c, k).wait_recv()
 
+    def line_stage(c, k):
+        line_arrives(c, k, is_inner)
         if k + 2 < planes:
             forward(c, k + 1)
 
@@ -347,6 +325,11 @@
         forward(c, 0)
 
     head = head_ref[0]
+
+    slots = planes * GROUP
+
+    def slot_of(at):
+        return at & (slots - 1) if slots & (slots - 1) == 0 else lax.rem(at, slots)
 
     def product(c, a, tile, table):
         total = None
@@ -355,12 +338,12 @@
             last = min(first + 2, count)
             spans = []
             for b in range(first, last):
-                base = head + 2 * planes * GROUP - table[a, 0, p * blocks + starts[c] + b]
+                base = head + 2 * slots - table[a, 0, p * blocks + starts[c] + b]
                 spans.append(
                     jnp.concatenate(
                         [
                             held[c][
-                                lax.rem(base + t, planes * GROUP),
+                                slot_of(base + t),
                                 :,
                                 b * block_cols : (b + 1) * block_cols,
                             ]
@@ -437,11 +420,6 @@
                 self.part_copy(off).wait_send()
 
     main = Sum(acc, pair, parts, pair_send, pair_recv, part_send, part_recv)
-    other = Sum(
-        other_acc, other_pair, other_parts,
-        other_pair_send, other_pair_recv, other_part_send, other_part_recv,
-    )
-
     def tiles_arrive(c):
         own_tile(c).wait()
         for off in range(1, GROUP):
@@ -449,6 +427,8 @@
 
     def compute(c):
         tiles_arrive(c)
+        for k in range(planes - 1):
+            line_arrives(c, k, is_end)
 
         def one(a):
             acc[a] += product(c, a, tiles[c], delay_smem)
@@ -457,61 +437,14 @@
             lax.fori_loop(0, GROUP, lambda a, carry: (one(a), carry)[1], 0)
         else:
             main.send(one)
-
-    def other_tile_copy(a, plane):
-        return remote(
-            tiles[0].at[a], other_tiles.at[a], other_tile_send.at[a], other_tile_recv.at[a], plane, p
-        )
-
-    def other_delay_copy(plane):
-        return remote(
-            delay_vmem, other_delay_vmem, other_delay_send, other_delay_recv, plane, p
-        )
-
-    def hand_over():
-        other_delay_copy(inward).start()
-        own_tile(0).wait()
-        other_tile_copy(p, inward).start()
-        for off in range(1, GROUP):
-            tile_arrival(0, off).wait_recv()
-            other_tile_copy(peer(off), inward).start()
-
-    def compute_other():
-        other_delay_copy(outward).wait_recv()
-        table = pltpu.make_async_copy(other_delay_vmem, other_delay_smem, delay_local)
-        table.start()
-        table.wait()
-        for a in range(GROUP):
-            other_tile_copy(a, outward).wait_recv()
-
-        def one(a):
-            other_acc[a] = product(0, a, other_tiles, other_delay_smem)
-
-        other.send(one)
-
-    def return_copy(plane):
-        return remote(handed, returned, return_send, return_recv, plane, p)
-
-    def return_other():
-        handed[...] = other.total()
-        return_copy(outward).start()
 
     for off in range(1, GROUP):
         delay_copy(off).start()
     own_delay = pltpu.make_async_copy(delay_ref, delay_vmem.at[p], delay_recv.at[p])
     own_delay.start()
     send_pieces(0)
-
-    @pl.when(is_end)
-    def _():
-        send_tiles(0)
-
     send_pieces(1)
-
-    @pl.when(is_inner)
-    def _():
-        send_tiles(0)
-
+    send_tiles(0)
     acc[...] = jnp.zeros_like(acc)
     for s in range(CHUNKS + planes - 1):
         if s < CHUNKS:
@@ -527,26 +460,13 @@
             table = pltpu.make_async_copy(delay_vmem, delay_smem, delay_local)
             table.start()
             table.wait()
-            pl.when(is_end)(hand_over)
         for k in range(planes - 1):
             if 0 <= s - 1 - k < CHUNKS:
                 line_stage(s - 1 - k, k)
-        if s == planes + 2:
-            pl.when(serves)(return_other)
-        c = s - planes + 1
-        if c == 0:
-            pl.when(is_inner)(functools.partial(compute, 0))
-        elif 0 < c < CHUNKS:
-            compute(c)
-        if s == planes:
-            pl.when(serves)(compute_other)
+        if 0 <= s - planes + 1 < CHUNKS:
+            compute(s - planes + 1)
 
     coupling[...] = main.total()
-
-    @pl.when(is_end)
-    def _():
-        return_copy(inward).wait_recv()
-        coupling[...] += returned[...]
 
     state = tuple(init_ref[i] for i in range(6))
     member = lax.broadcasted_iota(jnp.int32, (members, rows), 0)
@@ -617,17 +537,6 @@
         plane_copy(off).wait_send()
     main.finish()
 
-    @pl.when(is_end)
-    def _():
-        other_delay_copy(inward).wait_send()
-        for a in range(GROUP):
-            other_tile_copy(a, inward).wait_send()
-
-    @pl.when(serves)
-    def _():
-        other.finish()
-        return_copy(outward).wait_send()
-
     for off in range(1, planes):
         line_copy(off).wait_send()
     for c in range(CHUNKS):
@@ -635,11 +544,11 @@
             piece_copy(c, off).wait_send()
             tile_copy(c, off).wait_send()
         for k in range(planes - 1):
-            @pl.when(sends_up(c, k))
+            @pl.when(sends_up(k))
             def _(c=c, k=k):
                 up_copy(c, k).wait_send()
 
-            @pl.when(sends_down(c, k))
+            @pl.when(sends_down(k))
             def _(c=c, k=k):
                 down_copy(c, k).wait_send()
 
@@ -672,17 +581,9 @@
         + [
             pltpu.VMEM((GROUP, 1, delays.shape[1]), jnp.int32),
             pltpu.SMEM((GROUP, 1, delays.shape[1]), jnp.int32),
-            pltpu.VMEM((GROUP, 1, delays.shape[1]), jnp.int32),
-            pltpu.SMEM((GROUP, 1, delays.shape[1]), jnp.int32),
-            pltpu.VMEM((GROUP, rows, widths[0]), jnp.bfloat16),
             pltpu.VMEM((GROUP, count, rows), f32),
             pltpu.VMEM((CHIPS, count, rows), f32),
             pltpu.VMEM((CHIPS, count, rows), f32),
-            pltpu.VMEM((GROUP, count, rows), f32),
-            pltpu.VMEM((CHIPS, count, rows), f32),
-            pltpu.VMEM((CHIPS, count, rows), f32),
-            pltpu.VMEM((count, rows), f32),
-            pltpu.VMEM((count, rows), f32),
             pltpu.VMEM((count, rows), f32),
             pltpu.VMEM((count, rows), jnp.bfloat16),
             pltpu.VMEM((planes, GROUP, STEPS, sensors), f32),
@@ -704,16 +605,6 @@
             dma((CHIPS,)),
             dma((CHIPS,)),
             dma((CHIPS,)),
-            dma((CHIPS,)),
-            dma((CHIPS,)),
-            dma((CHIPS,)),
-            dma((CHIPS,)),
-            dma((GROUP,)),
-            dma((GROUP,)),
-            dma,
-            dma,
-            dma,
-            dma,
             dma((GROUP,)),
             dma((GROUP,)),
             dma((planes,)),

time: 288 us -> 262 us (0.910)
  Pallas kernels: 284 us -> 258 us
    pallas_call x1, Pallas kernels: 284 us -> 258 us  [fused_body(): pl.pallas_call(functools.partial(fused_kernel, planes), out_shape=(jax.Sh...]
where the time goes in v3:
time: 262 us
  Pallas kernels  258 us (98%)
  local copies, waits for them, and re-layouts  2.86 us (1%)
    pallas_call x1, Pallas kernels, fused_body(): pl.pallas_call(functools.partial(fused_kernel, planes), out_shape=(jax.Sh...  258 us

profile of v3, /device:TPU:0, one launch (start us, length us, event | category | flops | bytes accessed | tf_op | source)
XLA Modules:
  0.0 261.8 jit_solution(259915799417162304)
XLA Ops:
  1.3 257.7 %shard_map.86 = (f32[1,16,256]{2,1,0:T(8,128)}, f32[6,32,128]{2,1,0:T(8,128)}) custom-call(bf16[128,51200]{1,0:T(8,128)(2,1)} %conn_ref.1, bf16[1,32,51200]{2,1,0:T(8,128)(2,1)} %hist_ref.1, s32[1,400]{1,0:T(1,128)} %delay_ref.1, s32[1]{0:T(128)S(6)} %copy.11.head_ref, f32[32]{0:T(128)} %outside_ref.1, f32[6,32,128]{2,1,0:T(8,128)} %init_ref.1, ...), custom_call_target="tpu_custom_call" | custom-call | flops 6710886400 | bytes 26214400 | tf_op jit(solution)/shard_map/pallas_call | solution.py:571
  258.9 1.3 copy.12
  260.3 1.5 copy.13

commit v4 on v3

--- a/solution.py
+++ b/solution.py
@@ -331,36 +331,35 @@
     def slot_of(at):
         return at & (slots - 1) if slots & (slots - 1) == 0 else lax.rem(at, slots)
 
-    def product(c, a, tile, table):
-        total = None
+    def add_product(c, a):
         count = starts[c + 1] - starts[c]
-        for first in range(0, count, 2):
-            last = min(first + 2, count)
-            spans = []
-            for b in range(first, last):
-                base = head + 2 * slots - table[a, 0, p * blocks + starts[c] + b]
-                spans.append(
-                    jnp.concatenate(
-                        [
-                            held[c][
-                                slot_of(base + t),
-                                :,
-                                b * block_cols : (b + 1) * block_cols,
-                            ]
-                            for t in range(STEPS)
-                        ],
-                        axis=0,
+        half = STEPS // 2
+        for early in range(0, STEPS, half):
+            total = None
+            for first in range(0, count, 2):
+                last = min(first + 2, count)
+                spans = []
+                for b in range(first, last):
+                    base = head + 2 * slots - delay_smem[a, 0, p * blocks + starts[c] + b]
+                    spans.append(
+                        jnp.concatenate(
+                            [
+                                held[c][
+                                    slot_of(base + t), :, b * block_cols : (b + 1) * block_cols
+                                ]
+                                for t in range(early, early + half)
+                            ],
+                            axis=0,
+                        )
                     )
+                term = lax.dot_general(
+                    jnp.concatenate(spans, axis=1),
+                    tiles[c][a, :, first * block_cols : last * block_cols],
+                    (((1,), (1,)), ((), ())),
+                    preferred_element_type=jnp.float32,
                 )
-            window = jnp.concatenate(spans, axis=1)
-            term = lax.dot_general(
-                window,
-                tile[a, :, first * block_cols : last * block_cols],
-                (((1,), (1,)), ((), ())),
-                preferred_element_type=jnp.float32,
-            )
-            total = term if total is None else total + term
-        return total
+                total = term if total is None else total + term
+            acc[a, early * members : (early + half) * members, :] += total
 
     class Sum:
         def __init__(self, own, pair, parts, pair_send, pair_recv, part_send, part_recv):
@@ -431,7 +430,7 @@
             line_arrives(c, k, is_end)
 
         def one(a):
-            acc[a] += product(c, a, tiles[c], delay_smem)
+            add_product(c, a)
 
         if c < CHUNKS - 1:
             lax.fori_loop(0, GROUP, lambda a, carry: (one(a), carry)[1], 0)
@@ -442,17 +441,20 @@
         delay_copy(off).start()
     own_delay = pltpu.make_async_copy(delay_ref, delay_vmem.at[p], delay_recv.at[p])
     own_delay.start()
-    send_pieces(0)
-    send_pieces(1)
+    for c in range(3):
+        send_pieces(c)
     send_tiles(0)
+    send_tiles(1)
     acc[...] = jnp.zeros_like(acc)
     for s in range(CHUNKS + planes - 1):
-        if s < CHUNKS:
-            plane_stage(s)
-            if s + 2 < CHUNKS:
-                send_pieces(s + 2)
-            if s + 1 < CHUNKS:
-                send_tiles(s + 1)
+        if s == 0:
+            plane_stage(0)
+        if s + 3 < CHUNKS:
+            send_pieces(s + 3)
+        if s + 2 < CHUNKS:
+            send_tiles(s + 2)
+        if s + 1 < CHUNKS:
+            plane_stage(s + 1)
         if s == 0:
             own_delay.wait()
             for off in range(1, GROUP):

time: 262 us -> 286 us (1.092)
  Pallas kernels: 258 us -> 282 us
    pallas_call x1, Pallas kernels: 258 us -> 282 us  [fused_body(): pl.pallas_call(functools.partial(fused_kernel, planes), out_shape=(jax.Sh...]
where the time goes in v4:
time: 286 us
  Pallas kernels  282 us (99%)
  local copies, waits for them, and re-layouts  2.86 us (1%)
    pallas_call x1, Pallas kernels, fused_body(): pl.pallas_call(functools.partial(fused_kernel, planes), out_shape=(jax.Sh...  282 us

profile of v4, /device:TPU:0, one launch (start us, length us, event | category | flops | bytes accessed | tf_op | source)
XLA Modules:
  0.0 285.7 jit_solution(13893247984988946806)
XLA Ops:
  1.3 281.5 %shard_map.86 = (f32[1,16,256]{2,1,0:T(8,128)}, f32[6,32,128]{2,1,0:T(8,128)}) custom-call(bf16[128,51200]{1,0:T(8,128)(2,1)} %conn_ref.1, bf16[1,32,51200]{2,1,0:T(8,128)(2,1)} %hist_ref.1, s32[1,400]{1,0:T(1,128)} %delay_ref.1, s32[1]{0:T(128)S(6)} %copy.11.head_ref, f32[32]{0:T(128)} %outside_ref.1, f32[6,32,128]{2,1,0:T(8,128)} %init_ref.1, ...), custom_call_target="tpu_custom_call" | custom-call | flops 6710886400 | bytes 26214400 | tf_op jit(solution)/shard_map/pallas_call | solution.py:573
  282.8 1.3 copy.12
  284.1 1.5 copy.13

commit v5 on v3

--- a/solution.py
+++ b/solution.py
@@ -444,15 +444,13 @@
     own_delay.start()
     send_pieces(0)
     send_pieces(1)
-    send_tiles(0)
     acc[...] = jnp.zeros_like(acc)
     for s in range(CHUNKS + planes - 1):
         if s < CHUNKS:
             plane_stage(s)
             if s + 2 < CHUNKS:
                 send_pieces(s + 2)
-            if s + 1 < CHUNKS:
-                send_tiles(s + 1)
+            send_tiles(s)
         if s == 0:
             own_delay.wait()
             for off in range(1, GROUP):

time: 262 us -> 262 us (level)
  no operation moved by 1% of the time
where the time goes in v5:
time: 262 us
  Pallas kernels  258 us (98%)
  local copies, waits for them, and re-layouts  2.86 us (1%)
    pallas_call x1, Pallas kernels, fused_body(): pl.pallas_call(functools.partial(fused_kernel, planes), out_shape=(jax.Sh...  258 us

profile of v5, /device:TPU:0, one launch (start us, length us, event | category | flops | bytes accessed | tf_op | source)
XLA Modules:
  0.0 261.8 jit_solution(9355084972059821772)
XLA Ops:
  1.3 257.7 %shard_map.86 = (f32[1,16,256]{2,1,0:T(8,128)}, f32[6,32,128]{2,1,0:T(8,128)}) custom-call(bf16[128,51200]{1,0:T(8,128)(2,1)} %conn_ref.1, bf16[1,32,51200]{2,1,0:T(8,128)(2,1)} %hist_ref.1, s32[1,400]{1,0:T(1,128)} %delay_ref.1, s32[1]{0:T(128)S(6)} %copy.11.head_ref, f32[32]{0:T(128)} %outside_ref.1, f32[6,32,128]{2,1,0:T(8,128)} %init_ref.1, ...), custom_call_target="tpu_custom_call" | custom-call | flops 6710886400 | bytes 26214400 | tf_op jit(solution)/shard_map/pallas_call | solution.py:569
  258.9 1.3 copy.12
  260.3 1.5 copy.13
